TPU v7x, 32 devices: a whole 2x2x4 slice. The times are simulated.
32 devices in a mesh: gx: 4 (over z), gy: 8 (over y, x, core).
Axes of the slice: x: 2, y: 2, z: 4, core: 2. Of those that a mesh axis runs over, the one named last changes fastest.
Arguments:
- state: float32 [10, 32, 32768], P(None, None, ('gx', 'gy'))
- kdist: bfloat16 [224, 32], replicated, may hold values from 9.9658966e-05 to 0.049804688
- rayleigh: float32 [224], replicated, may hold values from 0.002 to 0.05
- solar: float32 [224], replicated, may hold values from 0.002 to 0.01
- span_map: int32 [32768], P(('gx', 'gy')), may hold values from 0 to 32767, as said below
- cos_zenith: float32 [32768], P(('gx', 'gy')), may hold values from -1 to 1, as said below
- day_flag: int32 [32768], P(('gx', 'gy')), may hold values from 0 to 1, as said below
- albedo: float32 [32768], P(('gx', 'gy')), may hold values from 0.05 to 0.8
Outputs:
- heating: float32 [32, 32768], P(None, ('gx', 'gy'))
- surface: float32 [3, 32768], P(None, ('gx', 'gy'))
Inputs may be any that keep to these rules, and one draw needn't show every extreme that they name: span_map is a permutation of the 32768 columns; a column held by device s (index in gx+gy order) goes to a column p with (p % 1024) // 32 == s, and each device's columns reach every device equally often. `cos_zenith`: column j of device d (index in gx+gy order) and column 1023 - j of the device whose index differs from d by 16 are antipodes: their values are opposite, of magnitude 0.05 or more. `day_flag`: 1 exactly where cos_zenith > 0.
All inputs are finite; a program needn't handle non-finite values.
Results may differ from a plain program's by a relative error of at most 0.00069.
Values sent between devices are 32-bit elements; how exact they have to be, the bound alone decides.
A program may use at most 64 MiB of HBM per device.

v0:
```python
import math

import jax
import jax.numpy as jnp
from jax import lax
from jax.sharding import PartitionSpec as P

diffusivity = 1.66
heat_factor = 8.0


def upward(carried, layer):
    albedo_below, source_below = carried
    reflect, transmit, direct_src = layer
    divisor = 1.0 - reflect * albedo_below
    albedo_top = reflect + transmit * transmit * albedo_below / divisor
    source_top = direct_src + transmit * (source_below + albedo_below * direct_src) / divisor
    return ((albedo_top, source_top), (albedo_below, source_below))


def downward(diffuse, layer):
    reflect, transmit, direct_src, albedo_below, source_below = layer
    lower_down = (transmit * diffuse + direct_src + reflect * source_below) / (
        1.0 - reflect * albedo_below
    )
    lower_up = albedo_below * lower_down + source_below
    return (lower_down, (lower_down, lower_up))


def column_physics(quantity_bundle, cosine, albedo, kdist, rayleigh, solar):
    levels = quantity_bundle.shape[1]
    columns = quantity_bundle.shape[2]
    kelvin_profile = quantity_bundle[0] / 250.0
    slab_weight_per_area = quantity_bundle[1]
    expansion_modes = jnp.stack(
        [
            jnp.ones_like(kelvin_profile),
            kelvin_profile,
            kelvin_profile * kelvin_profile,
            1.0 / kelvin_profile,
        ]
    )
    predictors = (quantity_bundle[2:, None] * expansion_modes[None] * slab_weight_per_area).astype(
        jnp.bfloat16
    )
    predictors = predictors.reshape(-1, levels, columns)
    block_width = math.gcd(kdist.shape[0], 32)
    blocks = kdist.shape[0] // block_width

    def one_block(block_index):
        start = block_index * block_width
        k_rows = lax.dynamic_slice_in_dim(kdist, start, block_width, 0)
        ray_rows = lax.dynamic_slice_in_dim(rayleigh, start, block_width, 0)
        sun_rows = lax.dynamic_slice_in_dim(solar, start, block_width, 0)
        tau_gas = jnp.einsum("gp,plc->lgc", k_rows, predictors, preferred_element_type=jnp.float32)
        tau_ray = ray_rows[None, :, None] * slab_weight_per_area[:, None, :]
        optical = tau_gas + tau_ray
        albedo_single = tau_ray / optical
        extinct = jnp.exp(-diffusivity * optical)
        reflect = 0.5 * albedo_single * (1.0 - extinct)
        transmit = extinct + reflect
        cumulative = jnp.cumsum(optical, axis=0)
        above = cumulative - optical
        direct_top = sun_rows[None, :, None] * cosine * jnp.exp(-above / cosine)
        direct_bottom = sun_rows[:, None] * cosine * jnp.exp(-cumulative[-1] / cosine)
        direct_src = 0.5 * albedo_single * (1.0 - jnp.exp(-optical / cosine)) * direct_top
        start_albedo = jnp.broadcast_to(albedo, direct_bottom.shape)
        (albedo_end, source_top), (albedo_below, source_below) = lax.scan(
            upward,
            (start_albedo, albedo * direct_bottom),
            (reflect, transmit, direct_src),
            reverse=True,
            unroll=True,
        )
        zeros = jnp.zeros_like(direct_bottom)
        final_down, (lower_down, lower_up) = lax.scan(
            downward,
            zeros,
            (reflect, transmit, direct_src, albedo_below, source_below),
            unroll=True,
        )
        direct_all = jnp.concatenate([direct_top, direct_bottom[None]], 0)
        down_all = jnp.concatenate([zeros[None], lower_down], 0)
        up_all = jnp.concatenate([source_top[None], lower_up], 0)
        net = jnp.sum(direct_all + down_all - up_all, axis=1)
        surface = jnp.stack(
            [jnp.sum(direct_bottom, 0), jnp.sum(final_down, 0), jnp.sum(source_top, 0)]
        )
        return (net, surface)

    nets, surfaces = lax.map(one_block, jnp.arange(blocks, dtype=jnp.int32))
    net = jnp.sum(nets, 0)
    heat_rate = heat_factor * (net[:-1] - net[1:]) / slab_weight_per_area
    return (heat_rate, jnp.sum(surfaces, 0))


def local(state, kdist, rayleigh, solar, span_map, cos_zenith, day_flag, albedo):
    columns = state.shape[-1]
    devices = lax.axis_size(("gx", "gy"))
    per_peer = columns // devices
    slot_index = span_map // columns * per_peer + span_map % per_peer
    daylit = day_flag.astype(jnp.float32)
    local_rows = jnp.stack([cos_zenith, albedo, daylit])
    arrived = lax.all_to_all(local_rows, ("gx", "gy"), split_axis=1, concat_axis=1, tiled=True)
    picked = jnp.take(arrived, slot_index, axis=1)
    cosine = jnp.where(picked[2] > 0.5, picked[0], jnp.float32(1.0))
    heat_rate, surface = column_physics(state, cosine, picked[1], kdist, rayleigh, solar)
    heating = heat_rate * picked[2]
    surface = surface * picked[2]
    outgoing = jnp.zeros_like(surface).at[:, slot_index].set(surface)
    surface = lax.all_to_all(outgoing, ("gx", "gy"), split_axis=1, concat_axis=1, tiled=True)
    return (heating, surface)


def solution(mesh):
    in_specs = (
        P(None, None, ("gx", "gy")),
        P(),
        P(),
        P(),
        P(("gx", "gy")),
        P(("gx", "gy")),
        P(("gx", "gy")),
        P(("gx", "gy")),
    )
    out_specs = (P(None, ("gx", "gy")), P(None, ("gx", "gy")))
    return jax.shard_map(local, mesh=mesh, in_specs=in_specs, out_specs=out_specs, check_vma=False)
```

profile of v0, /device:TPU:0, one launch (start us, length us, event | category | flops | bytes accessed | tf_op | source)
XLA Modules:
  0.0 419.6 jit_solution(13378130504580759408)
XLA Ops:
  3.7 7.3 %all-to-all-start = ((f32[3,32,32]{2,0,1:T(4,128)}), f32[3,32,32]{2,0,1:T(4,128)S(1)}, u32[]{:S(2)}, u32[]{:S(2)}) async-start(f32[3,32,32]{2,0,1:T(4,128)} %copy.38), calls=%async_computation | async-start | bytes 131072 | tf_op jit(solution)/shard_map/all_to_all | solution.py:104
  13.9 4.5 %all-to-all-done = f32[3,32,32]{2,0,1:T(4,128)S(1)} async-done(((f32[3,32,32]{2,0,1:T(4,128)}), f32[3,32,32]{2,0,1:T(4,128)S(1)}, u32[]{:S(2)}, u32[]{:S(2)}) %all-to-all-start) | async-done | bytes 12320 | tf_op jit(solution)/shard_map/all_to_all | solution.py:104
  18.7 2.8 gather_fusion
  23.1 378.4 %while.13 = (s32[]{:T(128)}, f32[7,33,1024]{2,1,0:T(8,128)}, f32[7,3,1024]{2,1,0:T(4,128)}, s32[7]{0:T(128)S(1)}, f32[224]{0:T(256)S(1)}, /*index=5*/f32[1024]{0...) while((s32[]{:T(128)}, f32[7,33,1024]{2,1,0:T(8,128)}, ...), condition=%wide.region_6.7_spmd.clone, body=%wide.region_0.6_spmd.clone.sunk | while | flops 147589120 | bytes 142224640 | solution.py:91
  24.5 3.2 broadcast_multiply_fusion.3
  27.6 5.4 %mul.2186 = f32[32,32,1024]{2,0,1:T(8,128)} reshape(f32[8,4,32,1024]{3,1,0,2:T(4,128)} %broadcast_multiply_fusion.3) | data formatting | bytes 8388608 | tf_op jit(solution)/shard_map/mul | solution.py:43
  33.0 3.0 multiply_add_fusion.2
  36.0 22.8 %fusion.40 = f32[32,32,1024]{2,1,0:T(8,128)S(1)} fusion(f32[32,32,1024]{2,1,0:T(8,128)S(1)} %multiply_add_fusion.2), kind=kOutput, calls=%fused_computation.354.clone.1 | output fusion | flops 32505856 | bytes 8388608 | tf_op jit(solution)/shard_map/while/body/eval_jaxpr/jit(cumsum)/reduce_window_sum | solution.py:62
  58.9 3.4 fusion.42
  63.9 3.4 fusion.43
  78.5 3.2 broadcast_multiply_fusion.3
  81.7 5.4 %mul.2186 = f32[32,32,1024]{2,0,1:T(8,128)} reshape(f32[8,4,32,1024]{3,1,0,2:T(4,128)} %broadcast_multiply_fusion.3) | data formatting | bytes 8388608 | tf_op jit(solution)/shard_map/mul | solution.py:43
  87.1 3.0 multiply_add_fusion.2
  90.1 22.8 %fusion.40 = f32[32,32,1024]{2,1,0:T(8,128)S(1)} fusion(f32[32,32,1024]{2,1,0:T(8,128)S(1)} %multiply_add_fusion.2), kind=kOutput, calls=%fused_computation.354.clone.1 | output fusion | flops 32505856 | bytes 8388608 | tf_op jit(solution)/shard_map/while/body/eval_jaxpr/jit(cumsum)/reduce_window_sum | solution.py:62
  113.0 3.4 fusion.42
  117.9 3.4 fusion.43
  132.6 3.2 broadcast_multiply_fusion.3
  135.8 5.4 %mul.2186 = f32[32,32,1024]{2,0,1:T(8,128)} reshape(f32[8,4,32,1024]{3,1,0,2:T(4,128)} %broadcast_multiply_fusion.3) | data formatting | bytes 8388608 | tf_op jit(solution)/shard_map/mul | solution.py:43
  141.1 3.0 multiply_add_fusion.2
  144.2 22.8 %fusion.40 = f32[32,32,1024]{2,1,0:T(8,128)S(1)} fusion(f32[32,32,1024]{2,1,0:T(8,128)S(1)} %multiply_add_fusion.2), kind=kOutput, calls=%fused_computation.354.clone.1 | output fusion | flops 32505856 | bytes 8388608 | tf_op jit(solution)/shard_map/while/body/eval_jaxpr/jit(cumsum)/reduce_window_sum | solution.py:62
  167.0 3.4 fusion.42
  172.0 3.4 fusion.43
  186.6 3.2 broadcast_multiply_fusion.3
  189.8 5.4 %mul.2186 = f32[32,32,1024]{2,0,1:T(8,128)} reshape(f32[8,4,32,1024]{3,1,0,2:T(4,128)} %broadcast_multiply_fusion.3) | data formatting | bytes 8388608 | tf_op jit(solution)/shard_map/mul | solution.py:43
  195.2 3.1 multiply_add_fusion.2
  198.2 22.8 %fusion.40 = f32[32,32,1024]{2,1,0:T(8,128)S(1)} fusion(f32[32,32,1024]{2,1,0:T(8,128)S(1)} %multiply_add_fusion.2), kind=kOutput, calls=%fused_computation.354.clone.1 | output fusion | flops 32505856 | bytes 8388608 | tf_op jit(solution)/shard_map/while/body/eval_jaxpr/jit(cumsum)/reduce_window_sum | solution.py:62
  221.1 3.4 fusion.42
  226.1 3.4 fusion.43
  240.7 3.2 broadcast_multiply_fusion.3
  243.9 5.4 %mul.2186 = f32[32,32,1024]{2,0,1:T(8,128)} reshape(f32[8,4,32,1024]{3,1,0,2:T(4,128)} %broadcast_multiply_fusion.3) | data formatting | bytes 8388608 | tf_op jit(solution)/shard_map/mul | solution.py:43
  249.3 3.0 multiply_add_fusion.2
  252.3 22.8 %fusion.40 = f32[32,32,1024]{2,1,0:T(8,128)S(1)} fusion(f32[32,32,1024]{2,1,0:T(8,128)S(1)} %multiply_add_fusion.2), kind=kOutput, calls=%fused_computation.354.clone.1 | output fusion | flops 32505856 | bytes 8388608 | tf_op jit(solution)/shard_map/while/body/eval_jaxpr/jit(cumsum)/reduce_window_sum | solution.py:62
  275.2 3.4 fusion.42
  280.1 3.4 fusion.43
  294.7 3.2 broadcast_multiply_fusion.3
  297.9 5.4 %mul.2186 = f32[32,32,1024]{2,0,1:T(8,128)} reshape(f32[8,4,32,1024]{3,1,0,2:T(4,128)} %broadcast_multiply_fusion.3) | data formatting | bytes 8388608 | tf_op jit(solution)/shard_map/mul | solution.py:43
  303.3 3.0 multiply_add_fusion.2
  306.3 22.8 %fusion.40 = f32[32,32,1024]{2,1,0:T(8,128)S(1)} fusion(f32[32,32,1024]{2,1,0:T(8,128)S(1)} %multiply_add_fusion.2), kind=kOutput, calls=%fused_computation.354.clone.1 | output fusion | flops 32505856 | bytes 8388608 | tf_op jit(solution)/shard_map/while/body/eval_jaxpr/jit(cumsum)/reduce_window_sum | solution.py:62
  329.2 3.4 fusion.42
  334.2 3.4 fusion.43
  348.8 3.2 broadcast_multiply_fusion.3
  352.0 5.4 %mul.2186 = f32[32,32,1024]{2,0,1:T(8,128)} reshape(f32[8,4,32,1024]{3,1,0,2:T(4,128)} %broadcast_multiply_fusion.3) | data formatting | bytes 8388608 | tf_op jit(solution)/shard_map/mul | solution.py:43
  357.4 3.0 multiply_add_fusion.2
  360.4 22.8 %fusion.40 = f32[32,32,1024]{2,1,0:T(8,128)S(1)} fusion(f32[32,32,1024]{2,1,0:T(8,128)S(1)} %multiply_add_fusion.2), kind=kOutput, calls=%fused_computation.354.clone.1 | output fusion | flops 32505856 | bytes 8388608 | tf_op jit(solution)/shard_map/while/body/eval_jaxpr/jit(cumsum)/reduce_window_sum | solution.py:62
  383.3 3.4 fusion.42
  388.2 3.4 fusion.43
  404.7 3.3 scatter_custom_fusion
  413.1 5.8 %all-to-all-done.1 = f32[3,32,32]{2,0,1:T(4,128)S(1)} async-done(((f32[3,32,32]{2,0,1:T(4,128)}), f32[3,32,32]{2,0,1:T(4,128)S(1)}, u32[]{:S(2)}, u32[]{:S(2)}) %all-to-all-start.1) | async-done | bytes 12320 | tf_op jit(solution)/shard_map/all_to_all | solution.py:111
  (567 shorter events, 99.7 us)
Async XLA Ops:
  0.6 12.6 %slice-start = ((f32[10,32,1024]{2,1,0:T(8,128)}), f32[8,32,1024]{2,1,0:T(8,128)S(1)}, s32[]{:S(2)}) async-start(f32[10,32,1024]{2,1,0:T(8,128)} %param.10), calls=%async_computation.2 | async-start | bytes 2097152 | tf_op jit(solution)/shard_map/slice | solution.py:43
  3.7 14.7 %all-to-all-start = ((f32[3,32,32]{2,0,1:T(4,128)}), f32[3,32,32]{2,0,1:T(4,128)S(1)}, u32[]{:S(2)}, u32[]{:S(2)}) async-start(f32[3,32,32]{2,0,1:T(4,128)} %copy.38), calls=%async_computation | async-start | bytes 131072 | tf_op jit(solution)/shard_map/all_to_all | solution.py:104
  12.8 9.9 %copy-start.16 = (bf16[224,32]{0,1:T(8,128)(2,1)S(1)}, bf16[224,32]{0,1:T(8,128)(2,1)}, u32[]{:S(2)}) copy-start(bf16[224,32]{0,1:T(8,128)(2,1)} %param.11) | copy-start | bytes 43012
  12.8 9.8 %copy-start.19 = (f32[224]{0:T(256)S(1)}, f32[224]{0:T(256)}, u32[]{:S(2)}) copy-start(f32[224]{0:T(256)} %param.13) | copy-start | bytes 2692
  12.9 9.8 %copy-start.20 = (f32[224]{0:T(256)S(1)}, f32[224]{0:T(256)}, u32[]{:S(2)}) copy-start(f32[224]{0:T(256)} %param.12) | copy-start | bytes 2692
  23.1 9.9 %copy-start.14 = (f32[32,1024]{1,0:T(8,128)}, f32[32,1024]{1,0:T(8,128)S(1)}, u32[]{:S(2)}) copy-start(f32[32,1024]{1,0:T(8,128)S(1)} %get-tuple-element.855) | copy-start | bytes 393220 | tf_op jit(solution)/shard_map/while
  67.3 5.9 %copy-start.3 = (f32[32,1024]{1,0:T(8,128)S(1)}, f32[32,1024]{1,0:T(8,128)}, u32[]{:S(2)}) copy-start(f32[32,1024]{1,0:T(8,128)} %get-tuple-element.724) | copy-start | bytes 393220 | tf_op jit(solution)/shard_map/while
  67.4 5.9 %copy-start.4 = (f32[32,1024]{1,0:T(8,128)S(1)}, f32[32,1024]{1,0:T(8,128)}, u32[]{:S(2)}) copy-start(f32[32,1024]{1,0:T(8,128)} %get-tuple-element.726) | copy-start | bytes 393220 | tf_op jit(solution)/shard_map/while
  67.4 6.0 %copy-start.1 = (f32[32,1024]{1,0:T(8,128)S(1)}, f32[32,1024]{1,0:T(8,128)}, u32[]{:S(2)}) copy-start(f32[32,1024]{1,0:T(8,128)} %get-tuple-element.728) | copy-start | bytes 393220 | tf_op jit(solution)/shard_map/while
  67.4 6.0 %copy-start.2 = (f32[32,1024]{1,0:T(8,128)S(1)}, f32[32,1024]{1,0:T(8,128)}, u32[]{:S(2)}) copy-start(f32[32,1024]{1,0:T(8,128)} %get-tuple-element.730) | copy-start | bytes 393220 | tf_op jit(solution)/shard_map/while
  67.4 6.0 %copy-start = (f32[32,1024]{1,0:T(8,128)S(1)}, f32[32,1024]{1,0:T(8,128)}, u32[]{:S(2)}) copy-start(f32[32,1024]{1,0:T(8,128)} %get-tuple-element.734) | copy-start | bytes 393220 | tf_op jit(solution)/shard_map/while
  77.1 9.9 %copy-start.14 = (f32[32,1024]{1,0:T(8,128)}, f32[32,1024]{1,0:T(8,128)S(1)}, u32[]{:S(2)}) copy-start(f32[32,1024]{1,0:T(8,128)S(1)} %get-tuple-element.855) | copy-start | bytes 393220 | tf_op jit(solution)/shard_map/while
  121.4 5.9 %copy-start.3 = (f32[32,1024]{1,0:T(8,128)S(1)}, f32[32,1024]{1,0:T(8,128)}, u32[]{:S(2)}) copy-start(f32[32,1024]{1,0:T(8,128)} %get-tuple-element.724) | copy-start | bytes 393220 | tf_op jit(solution)/shard_map/while
  121.4 5.9 %copy-start.4 = (f32[32,1024]{1,0:T(8,128)S(1)}, f32[32,1024]{1,0:T(8,128)}, u32[]{:S(2)}) copy-start(f32[32,1024]{1,0:T(8,128)} %get-tuple-element.726) | copy-start | bytes 393220 | tf_op jit(solution)/shard_map/while
  121.4 6.0 %copy-start.1 = (f32[32,1024]{1,0:T(8,128)S(1)}, f32[32,1024]{1,0:T(8,128)}, u32[]{:S(2)}) copy-start(f32[32,1024]{1,0:T(8,128)} %get-tuple-element.728) | copy-start | bytes 393220 | tf_op jit(solution)/shard_map/while
  121.4 6.0 %copy-start.2 = (f32[32,1024]{1,0:T(8,128)S(1)}, f32[32,1024]{1,0:T(8,128)}, u32[]{:S(2)}) copy-start(f32[32,1024]{1,0:T(8,128)} %get-tuple-element.730) | copy-start | bytes 393220 | tf_op jit(solution)/shard_map/while
  121.4 6.0 %copy-start = (f32[32,1024]{1,0:T(8,128)S(1)}, f32[32,1024]{1,0:T(8,128)}, u32[]{:S(2)}) copy-start(f32[32,1024]{1,0:T(8,128)} %get-tuple-element.734) | copy-start | bytes 393220 | tf_op jit(solution)/shard_map/while
  131.2 9.9 %copy-start.14 = (f32[32,1024]{1,0:T(8,128)}, f32[32,1024]{1,0:T(8,128)S(1)}, u32[]{:S(2)}) copy-start(f32[32,1024]{1,0:T(8,128)S(1)} %get-tuple-element.855) | copy-start | bytes 393220 | tf_op jit(solution)/shard_map/while
  175.5 5.9 %copy-start.3 = (f32[32,1024]{1,0:T(8,128)S(1)}, f32[32,1024]{1,0:T(8,128)}, u32[]{:S(2)}) copy-start(f32[32,1024]{1,0:T(8,128)} %get-tuple-element.724) | copy-start | bytes 393220 | tf_op jit(solution)/shard_map/while
  175.5 5.9 %copy-start.4 = (f32[32,1024]{1,0:T(8,128)S(1)}, f32[32,1024]{1,0:T(8,128)}, u32[]{:S(2)}) copy-start(f32[32,1024]{1,0:T(8,128)} %get-tuple-element.726) | copy-start | bytes 393220 | tf_op jit(solution)/shard_map/while
  175.5 6.0 %copy-start.1 = (f32[32,1024]{1,0:T(8,128)S(1)}, f32[32,1024]{1,0:T(8,128)}, u32[]{:S(2)}) copy-start(f32[32,1024]{1,0:T(8,128)} %get-tuple-element.728) | copy-start | bytes 393220 | tf_op jit(solution)/shard_map/while
  175.5 6.0 %copy-start.2 = (f32[32,1024]{1,0:T(8,128)S(1)}, f32[32,1024]{1,0:T(8,128)}, u32[]{:S(2)}) copy-start(f32[32,1024]{1,0:T(8,128)} %get-tuple-element.730) | copy-start | bytes 393220 | tf_op jit(solution)/shard_map/while
  175.5 6.0 %copy-start = (f32[32,1024]{1,0:T(8,128)S(1)}, f32[32,1024]{1,0:T(8,128)}, u32[]{:S(2)}) copy-start(f32[32,1024]{1,0:T(8,128)} %get-tuple-element.734) | copy-start | bytes 393220 | tf_op jit(solution)/shard_map/while
  185.2 9.9 %copy-start.14 = (f32[32,1024]{1,0:T(8,128)}, f32[32,1024]{1,0:T(8,128)S(1)}, u32[]{:S(2)}) copy-start(f32[32,1024]{1,0:T(8,128)S(1)} %get-tuple-element.855) | copy-start | bytes 393220 | tf_op jit(solution)/shard_map/while
  229.5 5.9 %copy-start.3 = (f32[32,1024]{1,0:T(8,128)S(1)}, f32[32,1024]{1,0:T(8,128)}, u32[]{:S(2)}) copy-start(f32[32,1024]{1,0:T(8,128)} %get-tuple-element.724) | copy-start | bytes 393220 | tf_op jit(solution)/shard_map/while
  229.5 5.9 %copy-start.4 = (f32[32,1024]{1,0:T(8,128)S(1)}, f32[32,1024]{1,0:T(8,128)}, u32[]{:S(2)}) copy-start(f32[32,1024]{1,0:T(8,128)} %get-tuple-element.726) | copy-start | bytes 393220 | tf_op jit(solution)/shard_map/while
  229.6 6.0 %copy-start.1 = (f32[32,1024]{1,0:T(8,128)S(1)}, f32[32,1024]{1,0:T(8,128)}, u32[]{:S(2)}) copy-start(f32[32,1024]{1,0:T(8,128)} %get-tuple-element.728) | copy-start | bytes 393220 | tf_op jit(solution)/shard_map/while
  229.6 6.0 %copy-start.2 = (f32[32,1024]{1,0:T(8,128)S(1)}, f32[32,1024]{1,0:T(8,128)}, u32[]{:S(2)}) copy-start(f32[32,1024]{1,0:T(8,128)} %get-tuple-element.730) | copy-start | bytes 393220 | tf_op jit(solution)/shard_map/while
  229.6 6.0 %copy-start = (f32[32,1024]{1,0:T(8,128)S(1)}, f32[32,1024]{1,0:T(8,128)}, u32[]{:S(2)}) copy-start(f32[32,1024]{1,0:T(8,128)} %get-tuple-element.734) | copy-start | bytes 393220 | tf_op jit(solution)/shard_map/while
  239.3 9.9 %copy-start.14 = (f32[32,1024]{1,0:T(8,128)}, f32[32,1024]{1,0:T(8,128)S(1)}, u32[]{:S(2)}) copy-start(f32[32,1024]{1,0:T(8,128)S(1)} %get-tuple-element.855) | copy-start | bytes 393220 | tf_op jit(solution)/shard_map/while
  283.6 5.9 %copy-start.3 = (f32[32,1024]{1,0:T(8,128)S(1)}, f32[32,1024]{1,0:T(8,128)}, u32[]{:S(2)}) copy-start(f32[32,1024]{1,0:T(8,128)} %get-tuple-element.724) | copy-start | bytes 393220 | tf_op jit(solution)/shard_map/while
  283.6 5.9 %copy-start.4 = (f32[32,1024]{1,0:T(8,128)S(1)}, f32[32,1024]{1,0:T(8,128)}, u32[]{:S(2)}) copy-start(f32[32,1024]{1,0:T(8,128)} %get-tuple-element.726) | copy-start | bytes 393220 | tf_op jit(solution)/shard_map/while
  283.6 6.0 %copy-start.1 = (f32[32,1024]{1,0:T(8,128)S(1)}, f32[32,1024]{1,0:T(8,128)}, u32[]{:S(2)}) copy-start(f32[32,1024]{1,0:T(8,128)} %get-tuple-element.728) | copy-start | bytes 393220 | tf_op jit(solution)/shard_map/while
  283.6 6.0 %copy-start.2 = (f32[32,1024]{1,0:T(8,128)S(1)}, f32[32,1024]{1,0:T(8,128)}, u32[]{:S(2)}) copy-start(f32[32,1024]{1,0:T(8,128)} %get-tuple-element.730) | copy-start | bytes 393220 | tf_op jit(solution)/shard_map/while
  283.6 6.0 %copy-start = (f32[32,1024]{1,0:T(8,128)S(1)}, f32[32,1024]{1,0:T(8,128)}, u32[]{:S(2)}) copy-start(f32[32,1024]{1,0:T(8,128)} %get-tuple-element.734) | copy-start | bytes 393220 | tf_op jit(solution)/shard_map/while
  293.4 9.9 %copy-start.14 = (f32[32,1024]{1,0:T(8,128)}, f32[32,1024]{1,0:T(8,128)S(1)}, u32[]{:S(2)}) copy-start(f32[32,1024]{1,0:T(8,128)S(1)} %get-tuple-element.855) | copy-start | bytes 393220 | tf_op jit(solution)/shard_map/while
  337.6 5.9 %copy-start.3 = (f32[32,1024]{1,0:T(8,128)S(1)}, f32[32,1024]{1,0:T(8,128)}, u32[]{:S(2)}) copy-start(f32[32,1024]{1,0:T(8,128)} %get-tuple-element.724) | copy-start | bytes 393220 | tf_op jit(solution)/shard_map/while
  337.7 5.9 %copy-start.4 = (f32[32,1024]{1,0:T(8,128)S(1)}, f32[32,1024]{1,0:T(8,128)}, u32[]{:S(2)}) copy-start(f32[32,1024]{1,0:T(8,128)} %get-tuple-element.726) | copy-start | bytes 393220 | tf_op jit(solution)/shard_map/while
  337.7 6.0 %copy-start.1 = (f32[32,1024]{1,0:T(8,128)S(1)}, f32[32,1024]{1,0:T(8,128)}, u32[]{:S(2)}) copy-start(f32[32,1024]{1,0:T(8,128)} %get-tuple-element.728) | copy-start | bytes 393220 | tf_op jit(solution)/shard_map/while
  337.7 6.0 %copy-start.2 = (f32[32,1024]{1,0:T(8,128)S(1)}, f32[32,1024]{1,0:T(8,128)}, u32[]{:S(2)}) copy-start(f32[32,1024]{1,0:T(8,128)} %get-tuple-element.730) | copy-start | bytes 393220 | tf_op jit(solution)/shard_map/while
  337.7 6.0 %copy-start = (f32[32,1024]{1,0:T(8,128)S(1)}, f32[32,1024]{1,0:T(8,128)}, u32[]{:S(2)}) copy-start(f32[32,1024]{1,0:T(8,128)} %get-tuple-element.734) | copy-start | bytes 393220 | tf_op jit(solution)/shard_map/while
  347.4 9.9 %copy-start.14 = (f32[32,1024]{1,0:T(8,128)}, f32[32,1024]{1,0:T(8,128)S(1)}, u32[]{:S(2)}) copy-start(f32[32,1024]{1,0:T(8,128)S(1)} %get-tuple-element.855) | copy-start | bytes 393220 | tf_op jit(solution)/shard_map/while
  391.7 5.9 %copy-start.3 = (f32[32,1024]{1,0:T(8,128)S(1)}, f32[32,1024]{1,0:T(8,128)}, u32[]{:S(2)}) copy-start(f32[32,1024]{1,0:T(8,128)} %get-tuple-element.724) | copy-start | bytes 393220 | tf_op jit(solution)/shard_map/while
  391.7 5.9 %copy-start.4 = (f32[32,1024]{1,0:T(8,128)S(1)}, f32[32,1024]{1,0:T(8,128)}, u32[]{:S(2)}) copy-start(f32[32,1024]{1,0:T(8,128)} %get-tuple-element.726) | copy-start | bytes 393220 | tf_op jit(solution)/shard_map/while
  391.7 6.0 %copy-start.1 = (f32[32,1024]{1,0:T(8,128)S(1)}, f32[32,1024]{1,0:T(8,128)}, u32[]{:S(2)}) copy-start(f32[32,1024]{1,0:T(8,128)} %get-tuple-element.728) | copy-start | bytes 393220 | tf_op jit(solution)/shard_map/while
  391.7 6.0 %copy-start.2 = (f32[32,1024]{1,0:T(8,128)S(1)}, f32[32,1024]{1,0:T(8,128)}, u32[]{:S(2)}) copy-start(f32[32,1024]{1,0:T(8,128)} %get-tuple-element.730) | copy-start | bytes 393220 | tf_op jit(solution)/shard_map/while
  391.7 6.0 %copy-start = (f32[32,1024]{1,0:T(8,128)S(1)}, f32[32,1024]{1,0:T(8,128)}, u32[]{:S(2)}) copy-start(f32[32,1024]{1,0:T(8,128)} %get-tuple-element.734) | copy-start | bytes 393220 | tf_op jit(solution)/shard_map/while
  408.9 10.0 %all-to-all-start.1 = ((f32[3,32,32]{2,0,1:T(4,128)}), f32[3,32,32]{2,0,1:T(4,128)S(1)}, u32[]{:S(2)}, u32[]{:S(2)}) async-start(f32[3,32,32]{2,0,1:T(4,128)} %copy.45), calls=%async_computation.1 | async-start | bytes 131072 | tf_op jit(solution)/shard_map/all_to_all | solution.py:111
  (72 other events, 352.3 us)
where the time goes:
time: 422 us; the launch traced here: 420 us
  other arithmetic  306 us (73%)
  local copies, waits for them, and re-layouts  64.1 us (15%)
  matrix products  21.2 us (5%)
  waiting for transfers between devices  10.3 us (2%)
  starting transfers between devices  9.86 us (2%)
  loops' own time  7.24 us (2%)
    another operation x7, other arithmetic, one_block(): cumulative = jnp.cumsum(optical, axis=0)  160 us
    while x217, other arithmetic  40.3 us
    mul x7, local copies, waits for them, and re-layouts, column_physics(): quantity_bundle[2:, None] * expansion_modes[None] * slab_weight_per_area  37.6 us
    add x7, other arithmetic, one_block(): transmit = extinct + reflect  23.8 us
    reduce_sum x7, other arithmetic, one_block(): jnp.sum(final_down, 0)  23.7 us
    mul x8, other arithmetic, column_physics(): quantity_bundle[2:, None] * expansion_modes[None] * slab_weight_per_area  23.2 us
    dot_general x7, matrix products, one_block(): jnp.einsum('gp,plc->lgc', k_rows, predictors, preferred_element_type=jnp....  21.2 us
    reduce_sum x7, other arithmetic, one_block(): net = jnp.sum(direct_all + down_all - up_all, axis=1)  12.4 us
  transfers between devices with their start and end apart: 2, of which 2 were waited for; matrix products, arithmetic and copies ran while one was open for 1% of the time, Pallas kernels for 0%

commit v1 on v0

v1 whole, which is shorter than its diff:
```python
import functools
import math

import jax
import jax.numpy as jnp
from jax import lax
from jax.experimental import pallas as pl
from jax.experimental.pallas import tpu as pltpu
from jax.sharding import PartitionSpec as P

diffusivity = 1.66
heat_factor = 8.0
LANES = 128
SUBS = 8
PACKS = (1, 2, 4)
LOG2E = math.log2(math.e)
f32 = jnp.float32
bf16 = jnp.bfloat16


def pieces(x, count):
    out = []
    for _ in range(count):
        part = x.astype(bf16)
        out.append(part)
        x = x - part.astype(f32)
    return out


def dot_t(a, b):
    return lax.dot_general(a, b, (((1,), (1,)), ((), ())), preferred_element_type=f32)


def dot(a, b):
    return jnp.dot(a, b, preferred_element_type=f32)


def physics_kernel(
    per_peer, state_ref, rows_ref, span_ref, kdist_ref, gray_ref, gsol_ref,
    heat_ref, surf_ref,
    tab_ref, wide_ref, ray_ref, sol_ref,
    pm_ref, ca_ref, kk_ref, comp_ref, mc_ref, rhs_ref, mt_ref, ct_ref,
    tau_ref, q_ref, v_ref, e_ref, a_ref, s_ref, net_ref,
):
    levels, cols = heat_ref.shape
    npred = 4 * (state_ref.shape[0] - 2)
    section = rhs_ref.shape[0] // PACKS[-1]
    g = kdist_ref.shape[1]
    gb = g // PACKS[-1]
    c_diff = -diffusivity * LOG2E
    lane_rows = cols // LANES
    lane = lax.broadcasted_iota(jnp.int32, (1, LANES), 1)

    tab_ref[...] = jnp.zeros_like(tab_ref)
    high, low = pieces(kdist_ref[...].astype(f32) * c_diff, 2)
    tab_ref[0:npred, 0:g] = high.astype(f32)
    tab_ref[npred:2 * npred, 0:g] = low.astype(f32)
    gray = gray_ref[...]
    rh, rm, rl = [part.astype(f32) for part in pieces(gray * c_diff, 3)]
    sub16g = lax.broadcasted_iota(jnp.int32, (16, g), 0)
    tail16 = jnp.zeros((16, g), f32)
    for i, row in enumerate((rh, rh, rm, rh, rl, rm, gray * (0.5 * c_diff), gsol_ref[...])):
        tail16 = jnp.where(sub16g == i, row, tail16)
    tab_ref[2 * npred:2 * npred + 16, 0:g] = tail16
    turned = jnp.transpose(tab_ref[...])
    wide_ref[...] = turned
    for col, ref in ((2 * npred + 6, ray_ref), (2 * npred + 7, sol_ref)):
        spread = jnp.broadcast_to(turned[:g, col:col + 1], (g, LANES))
        at = 0
        for r in PACKS:
            rows = g // r
            value = spread[:rows]
            for q in range(1, r):
                value = jnp.where(lane >= q * (LANES // r), spread[q * rows:(q + 1) * rows], value)
            ref[at:at + rows, :] = value
            at += rows

    t = state_ref[0] / 250.0
    m_all = state_ref[1]
    basis = (None, t, t * t, 1.0 / t)
    for i in range(npred // 4):
        gas = state_ref[2 + i]
        for b in range(4):
            value = gas if b == 0 else gas * basis[b]
            pm_ref[pl.ds((4 * i + b) * levels, levels), :] = (value * m_all).astype(bf16)
    for i, part in enumerate(pieces(m_all, 3)):
        pm_ref[pl.ds((npred + i) * levels, levels), :] = part

    cos_row = rows_ref[0:1, :]
    alb_row = rows_ref[1:2, :]
    day = (cos_row > 0.0).astype(f32)
    sub8 = lax.broadcasted_iota(jnp.int32, (SUBS, LANES), 0)
    day8 = jnp.zeros((SUBS, LANES), f32)
    for a in range(lane_rows):
        day8 = jnp.where(sub8 == a, day[:, a * LANES:(a + 1) * LANES], day8)
    r128 = lax.broadcasted_iota(jnp.int32, (LANES, LANES), 0)
    c128 = lax.broadcasted_iota(jnp.int32, (LANES, LANES), 1)
    tri = (r128 <= c128).astype(f32).astype(bf16)
    day8b = jnp.concatenate([day8, jnp.zeros_like(day8)], 0).astype(bf16)
    inner = dot(day8b, tri)[:SUBS]
    total = dot(day8b, jnp.ones((LANES, LANES), bf16))[:SUBS]
    before = jnp.zeros((SUBS, LANES), f32)
    for a in range(lane_rows - 1):
        before = before + jnp.where(sub8 > a, total[a:a + 1, :], 0.0)
    code = jnp.where(day8 > 0.5, inner + before, 0.0)
    n_day = jnp.sum(day8).astype(jnp.int32)
    for a in range(lane_rows):
        kk_ref[0:1, a * LANES:(a + 1) * LANES] = code[a:a + 1, :]
    high = jnp.floor(code * (1.0 / 32.0))
    low = code - 32.0 * high
    span = span_ref[...]
    slot = lax.div(span, cols) * per_peer + lax.rem(span, per_peer)
    pick_low = (
        (slot & (LANES - 1)) == lax.broadcasted_iota(jnp.int32, (LANES, cols), 0)
    ).astype(f32).astype(bf16)
    picked = dot(jnp.concatenate([high, low], 0).astype(bf16), pick_low)
    pick_high = (slot // LANES) == lax.broadcasted_iota(jnp.int32, (SUBS, cols), 0)
    merged = 32.0 * picked[:SUBS] + picked[SUBS:]
    kk_ref[1:2, :] = jnp.sum(jnp.where(pick_high, merged, 0.0), 0, keepdims=True)

    sub16 = lax.broadcasted_iota(jnp.int32, (16, cols), 0)
    ca = jnp.zeros((16, cols), f32)
    for i, part in enumerate(pieces(cos_row, 3) + pieces(alb_row, 3)):
        ca = jnp.where(sub16 == i, part.astype(f32), ca)
    ca_ref[...] = ca.astype(bf16)

    heat_ref[...] = jnp.zeros_like(heat_ref)
    surf_ref[...] = jnp.zeros_like(surf_ref)

    full = (n_day + 31) // LANES
    rem = jnp.maximum(n_day - full * LANES, 0)
    has64 = (rem > 32).astype(jnp.int32)
    has32 = (rem - 64 * has64 > 0).astype(jnp.int32)

    @pl.loop(0, full + has64 + has32)
    def chunk(c):
        is_full = c < full
        is_64 = jnp.logical_and(c == full, has64 == 1)
        width = jnp.where(is_full, LANES, jnp.where(is_64, LANES // 2, LANES // 4))
        base = jnp.where(
            is_full, c * LANES, full * LANES + jnp.where(is_64, 0, 64 * has64)
        )
        first = jnp.where(is_full, 0, jnp.where(is_64, 4, 6))
        count = jnp.where(is_full, 4, jnp.where(is_64, 2, 1))

        target = (
            base + 1 + (lax.broadcasted_iota(jnp.int32, (LANES, cols), 0) & (width - 1))
        ).astype(f32)
        ct_ref[...] = (kk_ref[0:1, :] == target).astype(f32).astype(bf16)
        mt_ref[...] = (kk_ref[1:2, :] == target).astype(f32).astype(bf16)
        comp_ref[...] = dot_t(pm_ref[...], mt_ref[...])
        column = lane & (width - 1)
        valid = base + column < n_day
        ca = dot_t(ca_ref[...], ct_ref[...])
        cosine = jnp.where(valid, ca[0:1] + ca[1:2] + ca[2:3], 1.0)
        albedo = ca[3:4] + ca[4:5] + ca[5:6]

        pack = lax.shift_right_logical(lane, jnp.where(is_full, 7, jnp.where(is_64, 6, 5)))
        m0 = npred * levels
        mh = jnp.where(valid, comp_ref[pl.ds(m0, levels), :], 1.0)
        mm = comp_ref[pl.ds(m0 + levels, levels), :]
        ml = comp_ref[pl.ds(m0 + 2 * levels, levels), :]
        mc_ref[...] = mh + mm + ml
        s16 = lax.broadcasted_iota(jnp.int32, (16, LANES), 0)

        def optics(r):
            for l in range(levels):
                optics_level(r, l)
            rows = g // r
            for l in range(0, levels, 2):
                two = sum(
                    dot(
                        wide_ref[q * rows:(q + 1) * rows, 0:section].astype(bf16),
                        rhs_ref[q * section:(q + 1) * section, l * LANES:(l + 2) * LANES],
                    )
                    for q in range(r)
                )
                tau_ref[l, 0:rows] = two[:, :LANES]
                tau_ref[l + 1, 0:rows] = two[:, LANES:]

        def optics_level(r, l):
            rr = jnp.where(s16 == 3, ml[l:l + 1], 0.0)
            rr = jnp.where((s16 == 1) | (s16 == 5), mm[l:l + 1], rr)
            rr = jnp.where((s16 == 0) | (s16 == 2) | (s16 == 4), mh[l:l + 1], rr)
            pred = comp_ref[pl.ds(l, npred, stride=levels), :]
            block = jnp.concatenate([pred, pred, rr], 0)
            for q in range(r):
                part = block if r == 1 else jnp.where(pack == q, block, 0.0)
                rhs_ref[q * section:(q + 1) * section, l * LANES:(l + 1) * LANES] = (
                    part.astype(bf16)
                )

        @pl.when(is_full)
        def _():
            optics(1)

        @pl.when(is_64)
        def _():
            optics(2)

        @pl.when(jnp.logical_not(jnp.logical_or(is_full, is_64)))
        def _():
            optics(4)

        net_ref[...] = jnp.zeros_like(net_ref)
        c_sun = 1.0 / (diffusivity * cosine)

        def fold(x):
            return jnp.sum(x.reshape(gb // SUBS, SUBS, LANES), 0)

        @pl.loop(0, count)
        def g_block(j):
            at = pl.multiple_of(j * gb, SUBS)
            table = pl.ds(pl.multiple_of((first + j) * gb, SUBS), gb)

            def up(i, carry):
                below_a, below_s = carry
                l = levels - 1 - i
                depth = tau_ref[l, pl.ds(at, gb), :]
                ray_m = ray_ref[table, :] * mc_ref[pl.ds(l, 1), :]
                half_w = ray_m * pl.reciprocal(depth, approx=True)
                ext = jnp.exp2(depth)
                sun = jnp.exp2(c_sun * depth)
                reflect = half_w - half_w * ext
                transmit = ext + reflect
                src = half_w - half_w * sun
                inv = pl.reciprocal(1.0 - reflect * below_a, approx=True)
                q = transmit * inv
                below_s_here = below_s * sun
                q_ref[l] = q
                v_ref[l] = (src + reflect * below_s_here) * inv
                e_ref[l] = sun
                a_ref[l] = below_a
                s_ref[l] = below_s
                next_a = reflect + (q * transmit) * below_a
                next_s = src + q * (below_s_here + below_a * src)
                return next_a, next_s

            start_a = jnp.broadcast_to(albedo, (gb, LANES))
            _, top_s = lax.fori_loop(0, levels, up, (start_a, start_a), unroll=8)

            direct = sol_ref[table, :] * cosine
            top_up = top_s * direct
            net_ref[0:SUBS, :] += fold(direct - top_up)

            def down(l, carry):
                diffuse, direct = carry
                diffuse = q_ref[l] * diffuse + direct * v_ref[l]
                direct = direct * e_ref[l]
                net = (direct + diffuse) - (a_ref[l] * diffuse + s_ref[l] * direct)
                rows = pl.ds(pl.multiple_of((l + 1) * SUBS, SUBS), SUBS)
                net_ref[rows, :] += fold(net)
                return diffuse, direct

            diffuse, direct = lax.fori_loop(
                0, levels, down, (jnp.zeros((gb, LANES), f32), direct), unroll=8
            )
            tail = (levels + 1) * SUBS
            net_ref[tail:tail + SUBS, :] += fold(direct)
            net_ref[tail + SUBS:tail + 2 * SUBS, :] += fold(diffuse)
            net_ref[tail + 2 * SUBS:tail + 3 * SUBS, :] += fold(top_up)

        upper = net_ref[pl.ds(0, levels, stride=SUBS), :]
        lower = net_ref[pl.ds(SUBS, levels, stride=SUBS), :]
        for s in range(1, SUBS):
            upper = upper + net_ref[pl.ds(s, levels, stride=SUBS), :]
            lower = lower + net_ref[pl.ds(SUBS + s, levels, stride=SUBS), :]
        heat = heat_factor * (upper - lower) / mc_ref[...]
        heat_ref[...] += sum(dot(part, mt_ref[...]) for part in pieces(heat, 2))
        tail = (levels + 1) * SUBS
        three = [
            jnp.sum(net_ref[tail + i * SUBS:tail + (i + 1) * SUBS, :], 0, keepdims=True)
            for i in range(3)
        ]
        surf8 = jnp.zeros((16, LANES), f32)
        for i in range(3):
            surf8 = jnp.where(s16 == i, three[i], surf8)
        surf_ref[...] += sum(dot(part, ct_ref[...]) for part in pieces(surf8, 2))[:SUBS]


def local(state, kdist, rayleigh, solar, span_map, cos_zenith, day_flag, albedo):
    fields, levels, columns = state.shape
    devices = lax.axis_size(("gx", "gy"))
    per_peer = columns // devices
    g, npred = kdist.shape
    gb = g // PACKS[-1]
    section = 2 * npred + 16
    local_rows = jnp.stack([cos_zenith, albedo])
    arrived = lax.all_to_all(local_rows, ("gx", "gy"), split_axis=1, concat_axis=1, tiled=True)
    vmem = pl.BlockSpec(memory_space=pltpu.VMEM)
    sweep = pltpu.VMEM((levels, gb, LANES), f32)
    heating, surface = pl.pallas_call(
        functools.partial(physics_kernel, per_peer),
        out_shape=(
            jax.ShapeDtypeStruct((levels, columns), f32),
            jax.ShapeDtypeStruct((SUBS, columns), f32),
        ),
        in_specs=[vmem] * 6,
        out_specs=(vmem, vmem),
        scratch_shapes=[
            pltpu.VMEM((LANES, -(-g // LANES) * LANES), f32),
            pltpu.VMEM((-(-g // LANES) * LANES, LANES), f32),
            pltpu.VMEM((gb * sum(PACKS), LANES), f32),
            pltpu.VMEM((gb * sum(PACKS), LANES), f32),
            pltpu.VMEM(((npred + 3) * levels, columns), bf16),
            pltpu.VMEM((16, columns), bf16),
            pltpu.VMEM((SUBS, columns), f32),
            pltpu.VMEM(((npred + 3) * levels, LANES), f32),
            pltpu.VMEM((levels, LANES), f32),
            pltpu.VMEM((PACKS[-1] * section, levels * LANES), bf16),
            pltpu.VMEM((LANES, columns), bf16),
            pltpu.VMEM((LANES, columns), bf16),
            pltpu.VMEM((levels, g, LANES), f32),
            sweep, sweep, sweep, sweep, sweep,
            pltpu.VMEM(((levels + 4) * SUBS, LANES), f32),
        ],
        compiler_params=pltpu.CompilerParams(vmem_limit_bytes=48 * 2**20),
    )(
        state, arrived, span_map.reshape(1, columns), kdist.T,
        rayleigh.reshape(1, g), solar.reshape(1, g),
    )
    surface = lax.all_to_all(surface[:3], ("gx", "gy"), split_axis=1, concat_axis=1, tiled=True)
    return (heating, surface)


def solution(mesh):
    in_specs = (
        P(None, None, ("gx", "gy")),
        P(),
        P(),
        P(),
        P(("gx", "gy")),
        P(("gx", "gy")),
        P(("gx", "gy")),
        P(("gx", "gy")),
    )
    out_specs = (P(None, ("gx", "gy")), P(None, ("gx", "gy")))
    return jax.shard_map(local, mesh=mesh, in_specs=in_specs, out_specs=out_specs, check_vma=False)
```

time: 422 us -> 65.7 us (0.16)
  other arithmetic: 306 us -> 0.04 us
  local copies, waits for them, and re-layouts: 64.1 us -> 6.54 us
  Pallas kernels: 0 us -> 35 us
  blocking collectives: 0 us -> 23.5 us
  matrix products: 21.2 us -> 0 us
  waiting for transfers between devices: 10.3 us -> 0 us
  starting transfers between devices: 9.86 us -> 0 us
  loops' own time: 7.24 us -> 0 us
    another operation x9 -> x1, other arithmetic: 160 us -> 0.04 us  [local(): local_rows = jnp.stack([cos_zenith, albedo])]
    while x217 -> x0, other arithmetic: 40.3 us -> none
    reduce_sum x30 -> x0, other arithmetic: 39.4 us -> none  [the longest x7 23.7 us: one_block(): jnp.sum(final_down, 0)]
    mul x8 -> x0, local copies, waits for them, and re-layouts: 37.9 us -> none  [the longest x7 37.6 us: column_physics(): quantity_bundle[2:, None] * expansion_modes[None] * slab_weight_per_area]
    pallas_call x0 -> x1, Pallas kernels: none -> 35 us  [local(): pl.pallas_call(functools.partial(physics_kernel, per_peer), out_shape=(ja...]
    add x21 -> x0, other arithmetic: 34.5 us -> none  [the longest x7 23.8 us: one_block(): transmit = extinct + reflect]
    mul x17 -> x0, other arithmetic: 26.2 us -> none  [the longest x8 23.2 us: column_physics(): quantity_bundle[2:, None] * expansion_modes[None] * slab_weight_per_area]
    all_to_all x0 -> x2, blocking collectives: none -> 23.5 us  [the longest x1 14.4 us: local(): lax.all_to_all(local_rows, ('gx', 'gy'), split_axis=1, concat_axis=1, til...]
  transfers between devices with their start and end apart: 2 -> 0, of which waited for: 2 -> 0; matrix products, arithmetic and copies ran while one was open for 1% -> 0% of each run, Pallas kernels for 0% -> 0%
where the time goes in v1:
time: 65.7 us
  Pallas kernels  35 us (53%)
  blocking collectives  23.5 us (36%)
  local copies, waits for them, and re-layouts  6.54 us (10%)
  between operations  0.67 us (1%)
    pallas_call x1, Pallas kernels, local(): pl.pallas_call(functools.partial(physics_kernel, per_peer), out_shape=(ja...  35 us
    all_to_all x1, blocking collectives, local(): lax.all_to_all(local_rows, ('gx', 'gy'), split_axis=1, concat_axis=1, til...  14.4 us
    all_to_all x1, blocking collectives, local(): lax.all_to_all(surface[:3], ('gx', 'gy'), split_axis=1, concat_axis=1, ti...  9.1 us
    unnamed x10, local copies, waits for them, and re-layouts  4.07 us
    another operation x2, local copies, waits for them, and re-layouts, local(): local_rows = jnp.stack([cos_zenith, albedo])  1.55 us

profile of v1, /device:TPU:0, one launch (start us, length us, event | category | flops | bytes accessed | tf_op | source)
XLA Modules:
  0.0 65.7 jit_solution(15744164279332389941)
XLA Ops:
  0.6 0.8 %stack.9 = f32[1,32,32]{2,0,1:T(1,128)S(1)} reshape(f32[1024]{0:T(1024)} %param.13) | data formatting | bytes 8192 | tf_op jit(solution)/shard_map/stack | solution.py:288
  1.4 0.8 %stack.10 = f32[1,32,32]{2,0,1:T(1,128)S(1)} reshape(f32[1024]{0:T(1024)} %param.14) | data formatting | bytes 8192 | tf_op jit(solution)/shard_map/stack | solution.py:288
  2.2 14.4 %all_to_all.20 = f32[2,32,32]{2,0,1:T(2,128)S(1)} all-to-all(f32[2,32,32]{2,0,1:T(2,128)S(1)} %pad_maximum_fusion), channel_id=1, replica_groups=mesh['gx'=4,'gy'=8] {'gx','gy'}, dimensions={1} | all-to-all | bytes 16384 | tf_op jit(solution)/shard_map/all_to_all | solution.py:289
  16.6 0.1 all_to_all.14.rows_ref
  16.7 0.0 copy-start
  16.7 1.3 %copy-done = f32[10,32,1024]{2,1,0:T(8,128)S(1)} copy-done((f32[10,32,1024]{2,1,0:T(8,128)S(1)}, f32[10,32,1024]{2,1,0:T(8,128)}, u32[]{:S(2)}) %copy-start) | copy-done | bytes 1310744
  18.0 0.0 copy-start.1
  18.0 0.7 %copy-done.1 = bf16[224,32]{0,1:T(8,128)(2,1)S(1)} copy-done((bf16[224,32]{0,1:T(8,128)(2,1)S(1)}, bf16[224,32]{0,1:T(8,128)(2,1)}, u32[]{:S(2)}) %copy-start.1) | copy-done | bytes 14360
  18.7 0.0 copy-start.2
  18.7 0.7 %copy-done.2 = s32[1024]{0:T(1024)S(1)} copy-done((s32[1024]{0:T(1024)S(1)}, s32[1024]{0:T(1024)}, u32[]{:S(2)}) %copy-start.2) | copy-done | bytes 4120
  19.4 0.0 copy-start.3
  19.4 0.7 %copy-done.3 = f32[224]{0:T(256)S(1)} copy-done((f32[224]{0:T(256)S(1)}, f32[224]{0:T(256)}, u32[]{:S(2)}) %copy-start.3) | copy-done | bytes 920
  20.1 0.0 copy-start.4
  20.1 0.7 %copy-done.4 = f32[224]{0:T(256)S(1)} copy-done((f32[224]{0:T(256)S(1)}, f32[224]{0:T(256)}, u32[]{:S(2)}) %copy-start.4) | copy-done | bytes 920
  20.8 35.0 %shard_map.86 = (f32[32,1024]{1,0:T(8,128)}, f32[8,1024]{1,0:T(8,128)S(1)}) custom-call(f32[10,32,1024]{2,1,0:T(8,128)S(1)} %copy-done, f32[2,1024]{1,0:T(2,128)S(1)} %all_to_all.14.rows_ref, s32[1,1024]{1,0:T(1,128)S(1)} %bitcast.5, bf16[32,224]{1,0:T(8,128)(2,1)S(1)} %bitcast.4, f32[1,224]{1,0:T(1,128)S(1)} %bitcast.6, f32[1,224]{1,0:T(1,128)S(1)} %bitcast.7), custom_call_target="tpu_custom_call" | custom-call | tf_op jit(solution)/shard_map/pallas_call | solution.py:292
  55.8 0.1 all_to_all.15
  55.9 9.1 %all_to_all.21 = f32[3,32,32]{2,0,1:T(4,128)S(1)} all-to-all(f32[3,32,32]{2,0,1:T(4,128)S(1)} %copy.12), channel_id=1, replica_groups=mesh['gx'=4,'gy'=8] {'gx','gy'}, dimensions={1} | all-to-all | bytes 24576 | tf_op jit(solution)/shard_map/all_to_all | solution.py:322
  65.0 0.7 %all_to_all.17 = f32[3,1024]{1,0:T(4,128)} reshape(f32[3,32,32]{2,1,0:T(8,128)S(1)} %copy.13) | data formatting | bytes 24576 | tf_op jit(solution)/shard_map/all_to_all | solution.py:322
  (5 shorter events, 0.1 us)
Async XLA Ops:
  16.7 1.3 %copy-start = (f32[10,32,1024]{2,1,0:T(8,128)S(1)}, f32[10,32,1024]{2,1,0:T(8,128)}, u32[]{:S(2)}) copy-start(f32[10,32,1024]{2,1,0:T(8,128)} %state_ref.1) | copy-start | bytes 3932164
  18.0 0.7 %copy-start.1 = (bf16[224,32]{0,1:T(8,128)(2,1)S(1)}, bf16[224,32]{0,1:T(8,128)(2,1)}, u32[]{:S(2)}) copy-start(bf16[224,32]{0,1:T(8,128)(2,1)} %param.9) | copy-start | bytes 43012
  18.7 0.7 %copy-start.2 = (s32[1024]{0:T(1024)S(1)}, s32[1024]{0:T(1024)}, u32[]{:S(2)}) copy-start(s32[1024]{0:T(1024)} %param.12) | copy-start | bytes 12292
  19.4 0.7 %copy-start.3 = (f32[224]{0:T(256)S(1)}, f32[224]{0:T(256)}, u32[]{:S(2)}) copy-start(f32[224]{0:T(256)} %param.10) | copy-start | bytes 2692
  20.1 0.7 %copy-start.4 = (f32[224]{0:T(256)S(1)}, f32[224]{0:T(256)}, u32[]{:S(2)}) copy-start(f32[224]{0:T(256)} %param.11) | copy-start | bytes 2692

commit v2 on v1

--- a/solution.py
+++ b/solution.py
@@ -36,15 +36,27 @@
 
 
 def physics_kernel(
-    per_peer, state_ref, rows_ref, span_ref, kdist_ref, gray_ref, gsol_ref,
+    per_peer, state_hbm, span_hbm, kdist_hbm, gray_hbm, gsol_hbm, rows_ref,
     heat_ref, surf_ref,
+    state_ref, span_ref, kdist_ref, gray_ref, gsol_ref, in_sem, basis_ref,
     tab_ref, wide_ref, ray_ref, sol_ref,
     pm_ref, ca_ref, kk_ref, comp_ref, mc_ref, rhs_ref, mt_ref, ct_ref,
-    tau_ref, q_ref, v_ref, e_ref, a_ref, s_ref, net_ref,
+    q_ref, v_ref, e_ref, a_ref, s_ref, net_ref,
 ):
     levels, cols = heat_ref.shape
     npred = 4 * (state_ref.shape[0] - 2)
-    section = rhs_ref.shape[0] // PACKS[-1]
+    section = rhs_ref.shape[1] // PACKS[-1]
+    fetch = [
+        pltpu.make_async_copy(src, dst, in_sem.at[i])
+        for i, (src, dst) in enumerate((
+            (kdist_hbm, kdist_ref), (gray_hbm, gray_ref), (gsol_hbm, gsol_ref),
+            (span_hbm, span_ref), (state_hbm, state_ref),
+        ))
+    ]
+    for copy in fetch:
+        copy.start()
+    for copy in fetch[:4]:
+        copy.wait()
     g = kdist_ref.shape[1]
     gb = g // PACKS[-1]
     c_diff = -diffusivity * LOG2E
@@ -52,7 +64,11 @@
     lane = lax.broadcasted_iota(jnp.int32, (1, LANES), 1)
 
     tab_ref[...] = jnp.zeros_like(tab_ref)
-    high, low = pieces(kdist_ref[...].astype(f32) * c_diff, 2)
+    kd = kdist_ref[...].astype(f32) * c_diff
+    kd = jnp.concatenate(
+        [kd[4 * i + b:4 * i + b + 1, :] for b in range(4) for i in range(npred // 4)], 0
+    )
+    high, low = pieces(kd, 2)
     tab_ref[0:npred, 0:g] = high.astype(f32)
     tab_ref[npred:2 * npred, 0:g] = low.astype(f32)
     gray = gray_ref[...]
@@ -74,17 +90,6 @@
                 value = jnp.where(lane >= q * (LANES // r), spread[q * rows:(q + 1) * rows], value)
             ref[at:at + rows, :] = value
             at += rows
-
-    t = state_ref[0] / 250.0
-    m_all = state_ref[1]
-    basis = (None, t, t * t, 1.0 / t)
-    for i in range(npred // 4):
-        gas = state_ref[2 + i]
-        for b in range(4):
-            value = gas if b == 0 else gas * basis[b]
-            pm_ref[pl.ds((4 * i + b) * levels, levels), :] = (value * m_all).astype(bf16)
-    for i, part in enumerate(pieces(m_all, 3)):
-        pm_ref[pl.ds((npred + i) * levels, levels), :] = part
 
     cos_row = rows_ref[0:1, :]
     alb_row = rows_ref[1:2, :]
@@ -124,6 +129,26 @@
         ca = jnp.where(sub16 == i, part.astype(f32), ca)
     ca_ref[...] = ca.astype(bf16)
 
+    fetch[4].wait()
+    ngas = npred // 4
+    t = state_ref[0] / 250.0
+    basis_ref[0] = t
+    basis_ref[1] = t * t
+    basis_ref[2] = 1.0 / t
+    m_all = state_ref[1]
+    for i, part in enumerate(pieces(m_all, 3)):
+        pm_ref[pl.ds((npred + i) * levels, levels), :] = part
+
+    @pl.loop(0, levels, unroll=4)
+    def level_predictors(l):
+        gas = state_ref[2:2 + ngas, pl.ds(l, 1), :].reshape(ngas, cols)
+        mass = state_ref[1, pl.ds(l, 1), :]
+        values = [gas * mass]
+        for b in range(3):
+            values.append(gas * basis_ref[b, pl.ds(l, 1), :] * mass)
+        rows = pl.ds(pl.multiple_of(l * npred, npred), npred)
+        pm_ref[rows, :] = jnp.concatenate(values, 0).astype(bf16)
+
     heat_ref[...] = jnp.zeros_like(heat_ref)
     surf_ref[...] = jnp.zeros_like(surf_ref)
 
@@ -132,91 +157,72 @@
     has64 = (rem > 32).astype(jnp.int32)
     has32 = (rem - 64 * has64 > 0).astype(jnp.int32)
 
-    @pl.loop(0, full + has64 + has32)
-    def chunk(c):
-        is_full = c < full
-        is_64 = jnp.logical_and(c == full, has64 == 1)
-        width = jnp.where(is_full, LANES, jnp.where(is_64, LANES // 2, LANES // 4))
-        base = jnp.where(
-            is_full, c * LANES, full * LANES + jnp.where(is_64, 0, 64 * has64)
-        )
-        first = jnp.where(is_full, 0, jnp.where(is_64, 4, 6))
-        count = jnp.where(is_full, 4, jnp.where(is_64, 2, 1))
-
+    s16 = lax.broadcasted_iota(jnp.int32, (16, LANES), 0)
+    m0 = npred * levels
+    c_gap = 1.0 / diffusivity
+
+    def chunk(r, base):
+        width = LANES // r
+        rows = g // r
+        first = gb * sum(PACKS[-1] // k for k in PACKS if k < r)
         target = (
             base + 1 + (lax.broadcasted_iota(jnp.int32, (LANES, cols), 0) & (width - 1))
         ).astype(f32)
         ct_ref[...] = (kk_ref[0:1, :] == target).astype(f32).astype(bf16)
         mt_ref[...] = (kk_ref[1:2, :] == target).astype(f32).astype(bf16)
         comp_ref[...] = dot_t(pm_ref[...], mt_ref[...])
-        column = lane & (width - 1)
-        valid = base + column < n_day
         ca = dot_t(ca_ref[...], ct_ref[...])
-        cosine = jnp.where(valid, ca[0:1] + ca[1:2] + ca[2:3], 1.0)
+        cosine = ca[0:1] + ca[1:2] + ca[2:3]
         albedo = ca[3:4] + ca[4:5] + ca[5:6]
-
-        pack = lax.shift_right_logical(lane, jnp.where(is_full, 7, jnp.where(is_64, 6, 5)))
-        m0 = npred * levels
-        mh = jnp.where(valid, comp_ref[pl.ds(m0, levels), :], 1.0)
-        mm = comp_ref[pl.ds(m0 + levels, levels), :]
-        ml = comp_ref[pl.ds(m0 + 2 * levels, levels), :]
-        mc_ref[...] = mh + mm + ml
-        s16 = lax.broadcasted_iota(jnp.int32, (16, LANES), 0)
-
-        def optics(r):
-            for l in range(levels):
-                optics_level(r, l)
-            rows = g // r
-            for l in range(0, levels, 2):
-                two = sum(
-                    dot(
-                        wide_ref[q * rows:(q + 1) * rows, 0:section].astype(bf16),
-                        rhs_ref[q * section:(q + 1) * section, l * LANES:(l + 2) * LANES],
-                    )
-                    for q in range(r)
-                )
-                tau_ref[l, 0:rows] = two[:, :LANES]
-                tau_ref[l + 1, 0:rows] = two[:, LANES:]
-
-        def optics_level(r, l):
-            rr = jnp.where(s16 == 3, ml[l:l + 1], 0.0)
-            rr = jnp.where((s16 == 1) | (s16 == 5), mm[l:l + 1], rr)
-            rr = jnp.where((s16 == 0) | (s16 == 2) | (s16 == 4), mh[l:l + 1], rr)
-            pred = comp_ref[pl.ds(l, npred, stride=levels), :]
-            block = jnp.concatenate([pred, pred, rr], 0)
+        mh = comp_ref[m0:m0 + levels, :]
+        valid = base + (lane & (width - 1)) < n_day
+        cosine = jnp.where(valid, cosine, 1.0)
+        mh = jnp.where(valid, mh, 1.0)
+        comp_ref[m0:m0 + levels, :] = mh
+        mc_ref[...] = (
+            mh + comp_ref[m0 + levels:m0 + 2 * levels, :]
+            + comp_ref[m0 + 2 * levels:m0 + 3 * levels, :]
+        )
+        pack = lane // width
+
+        @pl.loop(0, levels, unroll=4)
+        def right_side(l):
+            ph, pm, plow = [comp_ref[pl.ds(m0 + i * levels + l, 1), :] for i in range(3)]
+            rr = jnp.where(s16 == 3, plow, 0.0)
+            rr = jnp.where((s16 == 1) | (s16 == 5), pm, rr)
+            rr = jnp.where((s16 == 0) | (s16 == 2) | (s16 == 4), ph, rr)
+            pred = comp_ref[pl.ds(pl.multiple_of(l * npred, npred), npred), :]
             for q in range(r):
-                part = block if r == 1 else jnp.where(pack == q, block, 0.0)
-                rhs_ref[q * section:(q + 1) * section, l * LANES:(l + 1) * LANES] = (
-                    part.astype(bf16)
-                )
-
-        @pl.when(is_full)
-        def _():
-            optics(1)
-
-        @pl.when(is_64)
-        def _():
-            optics(2)
-
-        @pl.when(jnp.logical_not(jnp.logical_or(is_full, is_64)))
-        def _():
-            optics(4)
+                p, x = pred, rr
+                if r > 1:
+                    p = jnp.where(pack == q, p, 0.0)
+                    x = jnp.where(pack == q, x, 0.0)
+                p = p.astype(bf16)
+                at = q * section
+                rhs_ref[l, at:at + npred, :] = p
+                rhs_ref[l, at + npred:at + 2 * npred, :] = p
+                rhs_ref[l, at + 2 * npred:at + section, :] = x.astype(bf16)
 
         net_ref[...] = jnp.zeros_like(net_ref)
-        c_sun = 1.0 / (diffusivity * cosine)
+        c_sun = c_gap / cosine
 
         def fold(x):
             return jnp.sum(x.reshape(gb // SUBS, SUBS, LANES), 0)
 
-        @pl.loop(0, count)
+        @pl.loop(0, PACKS[-1] // r)
         def g_block(j):
-            at = pl.multiple_of(j * gb, SUBS)
-            table = pl.ds(pl.multiple_of((first + j) * gb, SUBS), gb)
+            table = pl.ds(pl.multiple_of(first + j * gb, SUBS), gb)
+            lhs = [
+                wide_ref[pl.ds(pl.multiple_of(q * rows + j * gb, SUBS), gb), 0:section].astype(bf16)
+                for q in range(r)
+            ]
 
             def up(i, carry):
                 below_a, below_s = carry
                 l = levels - 1 - i
-                depth = tau_ref[l, pl.ds(at, gb), :]
+                depth = sum(
+                    dot(lhs[q], rhs_ref[l, q * section:(q + 1) * section, :]) for q in range(r)
+                )
                 ray_m = ray_ref[table, :] * mc_ref[pl.ds(l, 1), :]
                 half_w = ray_m * pl.reciprocal(depth, approx=True)
                 ext = jnp.exp2(depth)
@@ -248,8 +254,8 @@
                 diffuse = q_ref[l] * diffuse + direct * v_ref[l]
                 direct = direct * e_ref[l]
                 net = (direct + diffuse) - (a_ref[l] * diffuse + s_ref[l] * direct)
-                rows = pl.ds(pl.multiple_of((l + 1) * SUBS, SUBS), SUBS)
-                net_ref[rows, :] += fold(net)
+                at = pl.ds(pl.multiple_of((l + 1) * SUBS, SUBS), SUBS)
+                net_ref[at, :] += fold(net)
                 return diffuse, direct
 
             diffuse, direct = lax.fori_loop(
@@ -277,6 +283,130 @@
             surf8 = jnp.where(s16 == i, three[i], surf8)
         surf_ref[...] += sum(dot(part, ct_ref[...]) for part in pieces(surf8, 2))[:SUBS]
 
+    @pl.loop(0, full)
+    def whole_chunks(c):
+        chunk(1, c * LANES)
+
+    @pl.when(has64 == 1)
+    def _():
+        chunk(2, full * LANES)
+
+    @pl.when(has32 == 1)
+    def _():
+        chunk(4, full * LANES + 64 * has64)
+
+
+def exchange_kernel(rows, n, gy_size, *refs):
+    count = (len(refs) - 6) // 2
+    ins = refs[count + 1:2 * count + 1]
+    out_ref = refs[count]
+    send_ref, recv_ref, send_sem, recv_sem, in_sem = refs[2 * count + 1:]
+    fetch = [
+        pltpu.make_async_copy(refs[i], ins[i], in_sem.at[i]) for i in range(count)
+    ]
+    for copy in fetch:
+        copy.start()
+    cols = out_ref.shape[1]
+    groups = cols // LANES
+    share = cols // n
+    per_group = LANES // share
+    me = lax.axis_index("gx") * gy_size + lax.axis_index("gy")
+
+    def device(d):
+        return (lax.div(d, gy_size), lax.rem(d, gy_size))
+
+    barrier = pltpu.get_barrier_semaphore()
+
+    def greet(i, _):
+        pl.semaphore_signal(
+            barrier, inc=1, device_id=device(lax.rem(me + i, n)),
+            device_id_type=pl.DeviceIdType.MESH,
+        )
+        return 0
+
+    lax.fori_loop(1, n, greet, 0)
+    send_ref[...] = jnp.zeros_like(send_ref)
+    for copy in fetch:
+        copy.wait()
+    for a in range(groups):
+        at = a * SUBS
+        for ref in ins:
+            count = min(ref.shape[0], rows)
+            send_ref[at:at + count, :] = ref[0:count, a * LANES:(a + 1) * LANES]
+            at += count
+    pl.semaphore_wait(barrier, n - 1)
+
+    def tile(i):
+        return pl.ds(pl.multiple_of(i * SUBS, SUBS), SUBS)
+
+    def outgoing(i):
+        d = lax.rem(me + i, n)
+        return pltpu.make_async_remote_copy(
+            src_ref=send_ref.at[tile(lax.div(d, per_group))],
+            dst_ref=recv_ref.at[tile(me)],
+            send_sem=send_sem.at[i],
+            recv_sem=recv_sem.at[i],
+            device_id=device(d),
+            device_id_type=pl.DeviceIdType.MESH,
+        )
+
+    def incoming(i):
+        d = lax.rem(me + n - i, n)
+        return pltpu.make_async_remote_copy(
+            src_ref=recv_ref.at[tile(d)],
+            dst_ref=recv_ref.at[tile(d)],
+            send_sem=send_sem.at[i],
+            recv_sem=recv_sem.at[i],
+            device_id=device(d),
+            device_id_type=pl.DeviceIdType.MESH,
+        )
+
+    def begin(i, _):
+        outgoing(i).start()
+        return 0
+
+    def end(i, _):
+        outgoing(i).wait_send()
+        incoming(i).wait_recv()
+        return 0
+
+    lax.fori_loop(1, n, begin, 0)
+    recv_ref[tile(me), :] = send_ref[tile(lax.div(me, per_group)), :]
+    lax.fori_loop(1, n, end, 0)
+
+    own = lax.rem(me, per_group) * share
+    place = lax.broadcasted_iota(jnp.int32, (groups, LANES), 1) // share
+    for r in range(rows):
+        merged = jnp.zeros((groups, LANES), f32)
+        for k in range(per_group):
+            part = recv_ref[pl.ds(k * SUBS + r, groups, stride=SUBS * per_group), :]
+            part = pltpu.roll(part, lax.rem(k * share + LANES - own, LANES), 1)
+            merged = jnp.where(place == k, part, merged)
+        for a in range(groups):
+            out_ref[r:r + 1, a * LANES:(a + 1) * LANES] = merged[a:a + 1, :]
+
+
+def exchange(inputs, rows, collective_id):
+    n = lax.axis_size(("gx", "gy"))
+    cols = inputs[0].shape[1]
+    vmem = pl.BlockSpec(memory_space=pltpu.VMEM)
+    return pl.pallas_call(
+        functools.partial(exchange_kernel, rows, n, lax.axis_size("gy")),
+        out_shape=jax.ShapeDtypeStruct((rows, cols), f32),
+        in_specs=[pl.BlockSpec(memory_space=pltpu.HBM)] * len(inputs),
+        out_specs=vmem,
+        scratch_shapes=[pltpu.VMEM(x.shape, f32) for x in inputs] + [
+            pltpu.VMEM((cols // LANES * SUBS, LANES), f32),
+            pltpu.VMEM((n * SUBS, LANES), f32),
+            pltpu.SemaphoreType.DMA((n,)),
+            pltpu.SemaphoreType.DMA((n,)),
+            pltpu.SemaphoreType.DMA((len(inputs),)),
+        ],
+        compiler_params=pltpu.CompilerParams(
+            collective_id=collective_id, has_side_effects=True, vmem_limit_bytes=60 * 2**20
+        ),
+    )(*inputs)
+
 
 def local(state, kdist, rayleigh, solar, span_map, cos_zenith, day_flag, albedo):
     fields, levels, columns = state.shape
@@ -285,8 +415,7 @@
     g, npred = kdist.shape
     gb = g // PACKS[-1]
     section = 2 * npred + 16
-    local_rows = jnp.stack([cos_zenith, albedo])
-    arrived = lax.all_to_all(local_rows, ("gx", "gy"), split_axis=1, concat_axis=1, tiled=True)
+    arrived = exchange([cos_zenith.reshape(1, columns), albedo.reshape(1, columns)], 2, 0)
     vmem = pl.BlockSpec(memory_space=pltpu.VMEM)
     sweep = pltpu.VMEM((levels, gb, LANES), f32)
     heating, surface = pl.pallas_call(
@@ -295,9 +424,16 @@
             jax.ShapeDtypeStruct((levels, columns), f32),
             jax.ShapeDtypeStruct((SUBS, columns), f32),
         ),
-        in_specs=[vmem] * 6,
+        in_specs=[pl.BlockSpec(memory_space=pltpu.HBM)] * 5 + [vmem],
         out_specs=(vmem, vmem),
         scratch_shapes=[
+            pltpu.VMEM(state.shape, f32),
+            pltpu.VMEM((1, columns), jnp.int32),
+            pltpu.VMEM((npred, g), bf16),
+            pltpu.VMEM((1, g), f32),
+            pltpu.VMEM((1, g), f32),
+            pltpu.SemaphoreType.DMA((5,)),
+            pltpu.VMEM((3, levels, columns), f32),
             pltpu.VMEM((LANES, -(-g // LANES) * LANES), f32),
             pltpu.VMEM((-(-g // LANES) * LANES, LANES), f32),
             pltpu.VMEM((gb * sum(PACKS), LANES), f32),
@@ -307,19 +443,18 @@
             pltpu.VMEM((SUBS, columns), f32),
             pltpu.VMEM(((npred + 3) * levels, LANES), f32),
             pltpu.VMEM((levels, LANES), f32),
-            pltpu.VMEM((PACKS[-1] * section, levels * LANES), bf16),
+            pltpu.VMEM((levels, PACKS[-1] * section, LANES), bf16),
             pltpu.VMEM((LANES, columns), bf16),
             pltpu.VMEM((LANES, columns), bf16),
-            pltpu.VMEM((levels, g, LANES), f32),
             sweep, sweep, sweep, sweep, sweep,
             pltpu.VMEM(((levels + 4) * SUBS, LANES), f32),
         ],
-        compiler_params=pltpu.CompilerParams(vmem_limit_bytes=48 * 2**20),
+        compiler_params=pltpu.CompilerParams(vmem_limit_bytes=56 * 2**20),
     )(
-        state, arrived, span_map.reshape(1, columns), kdist.T,
-        rayleigh.reshape(1, g), solar.reshape(1, g),
+        state, span_map.reshape(1, columns), kdist.T,
+        rayleigh.reshape(1, g), solar.reshape(1, g), arrived,
     )
-    surface = lax.all_to_all(surface[:3], ("gx", "gy"), split_axis=1, concat_axis=1, tiled=True)
+    surface = exchange([surface], 3, 1)
     return (heating, surface)
 
 

time: 65.7 us -> 64.5 us (0.982)
  Pallas kernels: 35 us -> 62.1 us
  blocking collectives: 23.5 us -> 0 us
  local copies, waits for them, and re-layouts: 6.54 us -> 1.33 us
    pallas_call x0 -> x2, Pallas kernels: none -> 25 us  [exchange(): pl.pallas_call(functools.partial(exchange_kernel, rows, n, lax.axis_size(...]
    all_to_all x2 -> x0, blocking collectives: 23.5 us -> none  [the longest x1 14.4 us: local(): lax.all_to_all(local_rows, ('gx', 'gy'), split_axis=1, concat_axis=1, til...]
    unnamed x10 -> x1, local copies, waits for them, and re-layouts: 4.07 us -> 1.33 us
    pallas_call x1, Pallas kernels: 35 us -> 37 us  [local(): pl.pallas_call(functools.partial(physics_kernel, per_peer), out_shape=(ja...]
    another operation x2 -> x0, local copies, waits for them, and re-layouts: 1.55 us -> none  [local(): local_rows = jnp.stack([cos_zenith, albedo])]
    all_to_all x6 -> x0, local copies, waits for them, and re-layouts: 0.91 us -> none  [the longest x4 0.83 us: local(): lax.all_to_all(surface[:3], ('gx', 'gy'), split_axis=1, concat_axis=1, ti...]
where the time goes in v2:
time: 64.5 us; the launch traced here: 64 us
  Pallas kernels  62.1 us (96%)
  local copies, waits for them, and re-layouts  1.33 us (2%)
  between operations  0.65 us (1%)
    pallas_call x1, Pallas kernels, local(): pl.pallas_call(functools.partial(physics_kernel, per_peer), out_shape=(ja...  37 us
    pallas_call x2, Pallas kernels, exchange(): pl.pallas_call(functools.partial(exchange_kernel, rows, n, lax.axis_size(...  25 us
    unnamed x1, local copies, waits for them, and re-layouts  1.33 us

profile of v2, /device:TPU:0, one launch (start us, length us, event | category | flops | bytes accessed | tf_op | source)
XLA Modules:
  0.0 64.0 jit_solution(17531712965224370277)
XLA Ops:
  0.6 11.5 %shard_map.86.rows_ref = f32[2,1024]{1,0:T(2,128)} custom-call(f32[1,1024]{1,0:T(1,128)} %bitcast.8, f32[1,1024]{1,0:T(1,128)} %bitcast.9), custom_call_target="tpu_custom_call" | custom-call | tf_op jit(solution)/shard_map/pallas_call | solution.py:393
  12.2 37.0 %shard_map.87 = (f32[32,1024]{1,0:T(8,128)}, f32[8,1024]{1,0:T(8,128)}) custom-call(f32[10,32,1024]{2,1,0:T(8,128)} %state_hbm.1, s32[1,1024]{1,0:T(1,128)} %bitcast.7, bf16[32,224]{1,0:T(8,128)(2,1)} %bitcast.6, f32[1,224]{1,0:T(1,128)} %bitcast.10, f32[1,224]{1,0:T(1,128)} %bitcast.11, f32[2,1024]{1,0:T(2,128)} %shard_map.86.rows_ref), custom_call_target="tpu_custom_call" | custom-call | tf_op jit(solution)/shard_map/pallas_call | solution.py:421
  49.2 13.5 %shard_map.88 = f32[3,1024]{1,0:T(4,128)} custom-call(f32[8,1024]{1,0:T(8,128)} %get-tuple-element.5.refs_0_), custom_call_target="tpu_custom_call" | custom-call | tf_op jit(solution)/shard_map/pallas_call | solution.py:393
  62.7 1.3 %copy.10 = f32[3,1024]{1,0:T(4,128)} copy(f32[3,1024]{1,0:T(4,128)} %shard_map.88) | data formatting | bytes 24576

commit v3 on v2

--- a/solution.py
+++ b/solution.py
@@ -41,7 +41,7 @@
     state_ref, span_ref, kdist_ref, gray_ref, gsol_ref, in_sem, basis_ref,
     tab_ref, wide_ref, ray_ref, sol_ref,
     pm_ref, ca_ref, kk_ref, comp_ref, mc_ref, rhs_ref, mt_ref, ct_ref,
-    q_ref, v_ref, e_ref, a_ref, s_ref, net_ref,
+    tau_ref, q_ref, v_ref, e_ref, a_ref, s_ref, net_ref,
 ):
     levels, cols = heat_ref.shape
     npred = 4 * (state_ref.shape[0] - 2)
@@ -185,13 +185,18 @@
         )
         pack = lane // width
 
-        @pl.loop(0, levels, unroll=4)
-        def right_side(l):
+        lhs = [
+            wide_ref[q * rows:(q + 1) * rows, 0:section].astype(bf16) for q in range(r)
+        ]
+
+        def right_side(pair, half):
+            l = 2 * pair + half
             ph, pm, plow = [comp_ref[pl.ds(m0 + i * levels + l, 1), :] for i in range(3)]
             rr = jnp.where(s16 == 3, plow, 0.0)
             rr = jnp.where((s16 == 1) | (s16 == 5), pm, rr)
             rr = jnp.where((s16 == 0) | (s16 == 2) | (s16 == 4), ph, rr)
             pred = comp_ref[pl.ds(pl.multiple_of(l * npred, npred), npred), :]
+            lanes = slice(half * LANES, (half + 1) * LANES)
             for q in range(r):
                 p, x = pred, rr
                 if r > 1:
@@ -199,9 +204,22 @@
                     x = jnp.where(pack == q, x, 0.0)
                 p = p.astype(bf16)
                 at = q * section
-                rhs_ref[l, at:at + npred, :] = p
-                rhs_ref[l, at + npred:at + 2 * npred, :] = p
-                rhs_ref[l, at + 2 * npred:at + section, :] = x.astype(bf16)
+                rhs_ref[pair, at:at + npred, lanes] = p
+                rhs_ref[pair, at + npred:at + 2 * npred, lanes] = p
+                rhs_ref[pair, at + 2 * npred:at + section, lanes] = x.astype(bf16)
+
+        @pl.loop(0, levels // 2, unroll=4)
+        def optics(pair):
+            right_side(pair, 0)
+            right_side(pair, 1)
+
+        @pl.loop(0, levels // 2, unroll=4)
+        def depths(pair):
+            two = sum(
+                dot(lhs[q], rhs_ref[pair, q * section:(q + 1) * section, :]) for q in range(r)
+            )
+            tau_ref[2 * pair, 0:rows] = two[:, :LANES]
+            tau_ref[2 * pair + 1, 0:rows] = two[:, LANES:]
 
         net_ref[...] = jnp.zeros_like(net_ref)
         c_sun = c_gap / cosine
@@ -212,17 +230,12 @@
         @pl.loop(0, PACKS[-1] // r)
         def g_block(j):
             table = pl.ds(pl.multiple_of(first + j * gb, SUBS), gb)
-            lhs = [
-                wide_ref[pl.ds(pl.multiple_of(q * rows + j * gb, SUBS), gb), 0:section].astype(bf16)
-                for q in range(r)
-            ]
+            own = pl.ds(pl.multiple_of(j * gb, SUBS), gb)
 
             def up(i, carry):
                 below_a, below_s = carry
                 l = levels - 1 - i
-                depth = sum(
-                    dot(lhs[q], rhs_ref[l, q * section:(q + 1) * section, :]) for q in range(r)
-                )
+                depth = tau_ref[l, own, :]
                 ray_m = ray_ref[table, :] * mc_ref[pl.ds(l, 1), :]
                 half_w = ray_m * pl.reciprocal(depth, approx=True)
                 ext = jnp.exp2(depth)
@@ -243,7 +256,7 @@
                 return next_a, next_s
 
             start_a = jnp.broadcast_to(albedo, (gb, LANES))
-            _, top_s = lax.fori_loop(0, levels, up, (start_a, start_a), unroll=8)
+            _, top_s = lax.fori_loop(0, levels, up, (start_a, start_a), unroll=16)
 
             direct = sol_ref[table, :] * cosine
             top_up = top_s * direct
@@ -259,7 +272,7 @@
                 return diffuse, direct
 
             diffuse, direct = lax.fori_loop(
-                0, levels, down, (jnp.zeros((gb, LANES), f32), direct), unroll=8
+                0, levels, down, (jnp.zeros((gb, LANES), f32), direct), unroll=16
             )
             tail = (levels + 1) * SUBS
             net_ref[tail:tail + SUBS, :] += fold(direct)
@@ -296,118 +309,6 @@
         chunk(4, full * LANES + 64 * has64)
 
 
-def exchange_kernel(rows, n, gy_size, *refs):
-    count = (len(refs) - 6) // 2
-    ins = refs[count + 1:2 * count + 1]
-    out_ref = refs[count]
-    send_ref, recv_ref, send_sem, recv_sem, in_sem = refs[2 * count + 1:]
-    fetch = [
-        pltpu.make_async_copy(refs[i], ins[i], in_sem.at[i]) for i in range(count)
-    ]
-    for copy in fetch:
-        copy.start()
-    cols = out_ref.shape[1]
-    groups = cols // LANES
-    share = cols // n
-    per_group = LANES // share
-    me = lax.axis_index("gx") * gy_size + lax.axis_index("gy")
-
-    def device(d):
-        return (lax.div(d, gy_size), lax.rem(d, gy_size))
-
-    barrier = pltpu.get_barrier_semaphore()
-
-    def greet(i, _):
-        pl.semaphore_signal(
-            barrier, inc=1, device_id=device(lax.rem(me + i, n)),
-            device_id_type=pl.DeviceIdType.MESH,
-        )
-        return 0
-
-    lax.fori_loop(1, n, greet, 0)
-    send_ref[...] = jnp.zeros_like(send_ref)
-    for copy in fetch:
-        copy.wait()
-    for a in range(groups):
-        at = a * SUBS
-        for ref in ins:
-            count = min(ref.shape[0], rows)
-            send_ref[at:at + count, :] = ref[0:count, a * LANES:(a + 1) * LANES]
-            at += count
-    pl.semaphore_wait(barrier, n - 1)
-
-    def tile(i):
-        return pl.ds(pl.multiple_of(i * SUBS, SUBS), SUBS)
-
-    def outgoing(i):
-        d = lax.rem(me + i, n)
-        return pltpu.make_async_remote_copy(
-            src_ref=send_ref.at[tile(lax.div(d, per_group))],
-            dst_ref=recv_ref.at[tile(me)],
-            send_sem=send_sem.at[i],
-            recv_sem=recv_sem.at[i],
-            device_id=device(d),
-            device_id_type=pl.DeviceIdType.MESH,
-        )
-
-    def incoming(i):
-        d = lax.rem(me + n - i, n)
-        return pltpu.make_async_remote_copy(
-            src_ref=recv_ref.at[tile(d)],
-            dst_ref=recv_ref.at[tile(d)],
-            send_sem=send_sem.at[i],
-            recv_sem=recv_sem.at[i],
-            device_id=device(d),
-            device_id_type=pl.DeviceIdType.MESH,
-        )
-
-    def begin(i, _):
-        outgoing(i).start()
-        return 0
-
-    def end(i, _):
-        outgoing(i).wait_send()
-        incoming(i).wait_recv()
-        return 0
-
-    lax.fori_loop(1, n, begin, 0)
-    recv_ref[tile(me), :] = send_ref[tile(lax.div(me, per_group)), :]
-    lax.fori_loop(1, n, end, 0)
-
-    own = lax.rem(me, per_group) * share
-    place = lax.broadcasted_iota(jnp.int32, (groups, LANES), 1) // share
-    for r in range(rows):
-        merged = jnp.zeros((groups, LANES), f32)
-        for k in range(per_group):
-            part = recv_ref[pl.ds(k * SUBS + r, groups, stride=SUBS * per_group), :]
-            part = pltpu.roll(part, lax.rem(k * share + LANES - own, LANES), 1)
-            merged = jnp.where(place == k, part, merged)
-        for a in range(groups):
-            out_ref[r:r + 1, a * LANES:(a + 1) * LANES] = merged[a:a + 1, :]
-
-
-def exchange(inputs, rows, collective_id):
-    n = lax.axis_size(("gx", "gy"))
-    cols = inputs[0].shape[1]
-    vmem = pl.BlockSpec(memory_space=pltpu.VMEM)
-    return pl.pallas_call(
-        functools.partial(exchange_kernel, rows, n, lax.axis_size("gy")),
-        out_shape=jax.ShapeDtypeStruct((rows, cols), f32),
-        in_specs=[pl.BlockSpec(memory_space=pltpu.HBM)] * len(inputs),
-        out_specs=vmem,
-        scratch_shapes=[pltpu.VMEM(x.shape, f32) for x in inputs] + [
-            pltpu.VMEM((cols // LANES * SUBS, LANES), f32),
-            pltpu.VMEM((n * SUBS, LANES), f32),
-            pltpu.SemaphoreType.DMA((n,)),
-            pltpu.SemaphoreType.DMA((n,)),
-            pltpu.SemaphoreType.DMA((len(inputs),)),
-        ],
-        compiler_params=pltpu.CompilerParams(
-            collective_id=collective_id, has_side_effects=True, vmem_limit_bytes=60 * 2**20
-        ),
-    )(*inputs)
-
-
 def local(state, kdist, rayleigh, solar, span_map, cos_zenith, day_flag, albedo):
     fields, levels, columns = state.shape
     devices = lax.axis_size(("gx", "gy"))
@@ -415,7 +316,9 @@
     g, npred = kdist.shape
     gb = g // PACKS[-1]
     section = 2 * npred + 16
-    arrived = exchange([cos_zenith.reshape(1, columns), albedo.reshape(1, columns)], 2, 0)
+    arrived = lax.all_to_all(
+        jnp.stack([cos_zenith, albedo]), ("gx", "gy"), split_axis=1, concat_axis=1, tiled=True
+    )
     vmem = pl.BlockSpec(memory_space=pltpu.VMEM)
     sweep = pltpu.VMEM((levels, gb, LANES), f32)
     heating, surface = pl.pallas_call(
@@ -443,9 +346,10 @@
             pltpu.VMEM((SUBS, columns), f32),
             pltpu.VMEM(((npred + 3) * levels, LANES), f32),
             pltpu.VMEM((levels, LANES), f32),
-            pltpu.VMEM((levels, PACKS[-1] * section, LANES), bf16),
+            pltpu.VMEM((levels // 2, PACKS[-1] * section, 2 * LANES), bf16),
             pltpu.VMEM((LANES, columns), bf16),
             pltpu.VMEM((LANES, columns), bf16),
+            pltpu.VMEM((levels, g, LANES), f32),
             sweep, sweep, sweep, sweep, sweep,
             pltpu.VMEM(((levels + 4) * SUBS, LANES), f32),
         ],
@@ -454,7 +358,7 @@
         state, span_map.reshape(1, columns), kdist.T,
         rayleigh.reshape(1, g), solar.reshape(1, g), arrived,
     )
-    surface = exchange([surface], 3, 1)
+    surface = lax.all_to_all(surface[:3], ("gx", "gy"), split_axis=1, concat_axis=1, tiled=True)
     return (heating, surface)
 
 

time: 64.5 us -> 69.8 us (1.082)
  blocking collectives: 0 us -> 27.9 us
  Pallas kernels: 62.1 us -> 37.1 us
  local copies, waits for them, and re-layouts: 1.33 us -> 3.82 us
    all_to_all x0 -> x2, blocking collectives: none -> 27.9 us  [the longest x1 14.4 us: local(): lax.all_to_all(jnp.stack([cos_zenith, albedo]), ('gx', 'gy'), split_axis=...]
    pallas_call x2 -> x0, Pallas kernels: 25 us -> none  [exchange(): pl.pallas_call(functools.partial(exchange_kernel, rows, n, lax.axis_size(...]
    another operation x0 -> x2, local copies, waits for them, and re-layouts: none -> 1.55 us  [local(): jnp.stack([cos_zenith, albedo])]
    all_to_all x0 -> x6, local copies, waits for them, and re-layouts: none -> 1.51 us  [the longest x4 0.82 us: local(): lax.all_to_all(surface[:3], ('gx', 'gy'), split_axis=1, concat_axis=1, ti...]
    unnamed x1 -> x0, local copies, waits for them, and re-layouts: 1.33 us -> none
    slice x0 -> x1, local copies, waits for them, and re-layouts: none -> 0.76 us  [local(): surface[:3]]
where the time goes in v3:
time: 69.8 us; the launch traced here: 69.6 us
  Pallas kernels  37.1 us (53%)
  blocking collectives  27.9 us (40%)
  local copies, waits for them, and re-layouts  3.82 us (5%)
    pallas_call x1, Pallas kernels, local(): pl.pallas_call(functools.partial(physics_kernel, per_peer), out_shape=(ja...  37.1 us
    all_to_all x1, blocking collectives, local(): lax.all_to_all(jnp.stack([cos_zenith, albedo]), ('gx', 'gy'), split_axis=...  14.4 us
    all_to_all x1, blocking collectives, local(): lax.all_to_all(surface[:3], ('gx', 'gy'), split_axis=1, concat_axis=1, ti...  13.6 us
    another operation x2, local copies, waits for them, and re-layouts, local(): jnp.stack([cos_zenith, albedo])  1.55 us

profile of v3, /device:TPU:0, one launch (start us, length us, event | category | flops | bytes accessed | tf_op | source)
XLA Modules:
  0.0 69.6 jit_solution(16568477275125053120)
XLA Ops:
  0.6 0.8 %stack.9 = f32[1,32,32]{2,0,1:T(1,128)S(1)} reshape(f32[1024]{0:T(1024)} %param.13) | data formatting | bytes 8192 | tf_op jit(solution)/shard_map/stack | solution.py:320
  1.4 0.8 %stack.10 = f32[1,32,32]{2,0,1:T(1,128)S(1)} reshape(f32[1024]{0:T(1024)} %param.14) | data formatting | bytes 8192 | tf_op jit(solution)/shard_map/stack | solution.py:320
  2.2 14.4 %all_to_all.20 = f32[2,32,32]{2,0,1:T(2,128)S(1)} all-to-all(f32[2,32,32]{2,0,1:T(2,128)S(1)} %pad_maximum_fusion), channel_id=1, replica_groups=mesh['gx'=4,'gy'=8] {'gx','gy'}, dimensions={1} | all-to-all | bytes 16384 | tf_op jit(solution)/shard_map/all_to_all | solution.py:319
  16.6 0.7 all_to_all.14.rows_ref
  17.3 37.1 %shard_map.86 = (f32[32,1024]{1,0:T(8,128)}, f32[8,1024]{1,0:T(8,128)}) custom-call(f32[10,32,1024]{2,1,0:T(8,128)} %state_hbm.1, s32[1,1024]{1,0:T(1,128)} %bitcast.5, bf16[32,224]{1,0:T(8,128)(2,1)} %bitcast.4, f32[1,224]{1,0:T(1,128)} %bitcast.6, f32[1,224]{1,0:T(1,128)} %bitcast.7, f32[2,1024]{1,0:T(2,128)} %all_to_all.14.rows_ref), custom_call_target="tpu_custom_call" | custom-call | tf_op jit(solution)/shard_map/pallas_call | solution.py:324
  54.4 0.8 %slice.3 = f32[3,1024]{1,0:T(4,128)S(1)} slice(f32[8,1024]{1,0:T(8,128)} %get-tuple-element.5), slice={[0:3], [0:1024]} | slice | bytes 24576 | tf_op jit(solution)/shard_map/slice | solution.py:361
  55.2 0.1 all_to_all.15
  55.3 13.6 %all_to_all.21 = f32[3,32,32]{2,0,1:T(4,128)S(1)} all-to-all(f32[3,32,32]{2,0,1:T(4,128)S(1)} %copy.12), channel_id=1, replica_groups=mesh['gx'=4,'gy'=8] {'gx','gy'}, dimensions={1} | all-to-all | bytes 24576 | tf_op jit(solution)/shard_map/all_to_all | solution.py:361
  68.9 0.7 %all_to_all.17 = f32[3,1024]{1,0:T(4,128)} reshape(f32[3,32,32]{2,1,0:T(8,128)S(1)} %copy.13) | data formatting | bytes 24576 | tf_op jit(solution)/shard_map/all_to_all | solution.py:361
  (4 shorter events, 0.1 us)
